TPU v7x, 128 devices: a whole 4x4x4 slice. The times are simulated.
128 devices in a mesh: dip: 64 (over y, z, x_hi, core), rep: 2 (over x_lo).
Axes of the slice: x: 4 (x_hi: 2, x_lo: 2; x = x_hi * 2 + x_lo), y: 4, z: 4, core: 2. Of those that a mesh axis runs over, the one named last changes fastest.
Arguments:
- slip_field: float32 [4096, 8192], P('dip', 'rep'), may hold values from -4 to 4
- state_field: float32 [4096, 8192], P('dip', 'rep'), may hold values from 0.5 to 2
- direct_effect: float32 [4096, 8192], P('dip', 'rep'), may hold values from 1 to 2
- load_stress: float32 [4096, 8192], P('dip', 'rep'), may hold values from -1 to 1
- kernel_spectrum: float32 [8192, 8192], P(('dip', 'rep')), may hold values from -0.5 to 0.5
Outputs:
- velocity: float32 [4096, 8192], P('dip', 'rep')
- state_next: float32 [4096, 8192], P('dip', 'rep')
All inputs are finite; a program needn't handle non-finite values.
Results may differ from a plain program's by a relative error of at most 0.00005.
Values sent between devices are 32-bit elements; how exact they have to be, the bound alone decides.
A program may use at most 128 MiB of HBM per device.

v0:
```python
import functools

import jax
import jax.numpy as jnp
import ml_dtypes
import numpy as np
from jax import lax
from jax.experimental import pallas as pl
from jax.experimental.pallas import tpu as pltpu
from jax.sharding import PartitionSpec as P

MESH = pl.DeviceIdType.MESH
F32 = jnp.float32
BF16 = jnp.bfloat16

time_step = 0.5
state_exponent = 0.8

ND = 4096
NS = 8192
COUNT = 128
LINES = 32
SLOTS = 32
CHUNKS = 2
QUADS = SLOTS // 4 // CHUNKS
ROWS = 2 * QUADS


def wave(product, period):
    angle = 2.0 * np.pi * (np.asarray(product, np.float64) / period)
    return np.cos(angle), np.sin(angle)


def halves(table):
    high = table.astype(ml_dtypes.bfloat16)
    low = (table - high.astype(np.float64)).astype(ml_dtypes.bfloat16)
    return high, low


def tables():
    out = {}
    f32 = np.float32
    v0 = np.arange(64)
    n1 = np.arange(64)
    n0 = np.arange(128)
    cos, sin = wave(np.outer(v0, n1), 64)
    high, low = halves(np.concatenate([cos, -sin], 0))
    out["t1"] = np.concatenate([high, high, low], 1)
    cos, sin = wave(np.outer(v0, n0), 8192)
    out["tw1c"], out["tw1s"] = cos.astype(f32), sin.astype(f32)
    for name, v1 in (("t2a", np.arange(64)), ("t2b", np.arange(63, -1, -1))):
        cos, sin = wave(np.outer(v1, n0), 128)
        full = np.concatenate(
            [np.concatenate([cos, sin], 1), np.concatenate([-sin, cos], 1)], 0
        )
        out[name] = np.concatenate(halves(full), 0)
        back = np.concatenate(
            [np.concatenate([cos, sin], 1), np.concatenate([-sin, cos], 1)], 0
        )
        high, low = halves(back)
        out[name.replace("t2", "t7")] = np.concatenate([high, high, low], 0)
    alt = np.zeros((64, 128))
    alt[0] = 1.0 - 2.0 * (n0 % 2)
    out["alt"] = alt.astype(ml_dtypes.bfloat16)
    s = np.arange(128)
    u0 = np.arange(256)
    u1 = np.arange(16)
    k = np.arange(32) + 0.5
    cos, sin = wave(np.outer(u0, s), 256)
    high, low = halves(np.concatenate([cos, -sin], 0))
    out["t3"] = np.concatenate([high, high, low], 1)
    cos, sin = wave(np.outer(u0, k), 8192)
    out["tw3c"], out["tw3s"] = np.tile(cos, (1, 4)).astype(f32), np.tile(sin, (1, 4)).astype(f32)
    cos, sin = wave(np.outer(u1, k), 32)
    eye = np.eye(4)
    full = np.concatenate([np.kron(eye, cos), np.kron(eye, sin)], 1)
    out["t4"] = np.concatenate(halves(full), 0)
    cos, sin = np.kron(eye, cos.T), np.kron(eye, sin.T)
    full = np.concatenate([np.concatenate([cos, -sin], 1), np.concatenate([sin, cos], 1)], 0)
    high, low = halves(full)
    out["t5"] = np.concatenate([high, high, low], 1)
    cos, sin = wave(np.outer(k, u0), 8192)
    out["tw5c"], out["tw5s"] = np.tile(cos, (4, 1)).astype(f32), np.tile(sin, (4, 1)).astype(f32)
    cos, sin = wave(np.outer(s, u0), 256)
    out["t6"] = np.concatenate(halves(np.concatenate([cos, -sin], 1)), 0)
    flip = np.zeros((256, 256))
    flip[(256 - u0) % 256, u0] = 1.0
    out["flip"] = flip.astype(ml_dtypes.bfloat16)
    cos, sin = wave(np.outer(n1, v0), 64)
    high, low = halves(np.concatenate([cos, -sin], 1))
    out["t8"] = np.concatenate([high, high, low], 1)
    return out


def split(value):
    high = value.astype(BF16)
    low = (value - high.astype(F32)).astype(BF16)
    return high, low


def dot(a, b):
    return lax.dot_general(a, b, (((1,), (0,)), ((), ())), preferred_element_type=F32)


def dot_t(a, b):
    return lax.dot_general(a, b, (((1,), (1,)), ((), ())), preferred_element_type=F32)


def table_dot(table, value):
    high, low = split(value)
    return dot(table, jnp.concatenate([high, low, high], 0))


def table_dot_t(table, value):
    high, low = split(value)
    rows = table.shape[0] // 2
    both = dot_t(table, high)
    return both[:rows] + both[rows:] + dot_t(table[:rows], low)


NAMES = (
    ("t1", "tw1c", "tw1s", "t2a", "t2b", "t7a", "t7b", "alt", "t8")
    + ("t3", "tw3c", "tw3s", "t4", "t5", "tw5c", "tw5s", "t6", "flip")
)


def body(slip, spectrum, *refs):
    count = len(NAMES)
    elastic = refs[count]
    tab = dict(zip(NAMES, refs[count + 1 : 2 * count + 1]))
    staged = {
        name: pltpu.make_async_copy(refs[i], tab[name], refs[2 * count + 1].at[i])
        for i, name in enumerate(NAMES)
    }
    (
        xin, xr, yr, yi, snd, rcv, pos, neg, edge,
        pd, pr, nd, nr, a_re, a_im, b_all, snd2, rcv2, ebuf, xout, sems, chunk_sems, out_sems,
    ) = refs[2 * count + 2 :]
    rep = lax.axis_index("rep")
    me = lax.axis_index("dip") * 2 + rep
    barrier = pltpu.get_barrier_semaphore()

    def place(other):
        return (other // 2, other % 2)

    def partner(step):
        mixed = lax.rem(step * 37, COUNT - 1)
        return jnp.bitwise_xor(me, jnp.where(mixed == 0, COUNT - 1, mixed))

    def greet(step, carry):
        pl.semaphore_signal(
            barrier, inc=1, device_id=place(partner(step)), device_id_type=MESH
        )
        return carry

    lax.fori_loop(1, COUNT, greet, 0)

    for name in NAMES:
        staged[name].start()
    own_slip = pltpu.make_async_copy(slip.at[pl.ds(rep * LINES, LINES)], xin.at[rep], sems.at[0])
    own_slip.start()
    low_side = me < COUNT // 2
    own_k_pos = pltpu.make_async_copy(spectrum.at[pl.ds(0, SLOTS)], pos, sems.at[1])
    own_k_neg = pltpu.make_async_copy(spectrum.at[pl.ds(0, SLOTS)], neg, sems.at[1])
    own_edge = pltpu.make_async_copy(spectrum.at[pl.ds(SLOTS, 1)], edge, sems.at[2])

    @pl.when(low_side)
    def _():
        own_k_pos.start()

    @pl.when(jnp.logical_not(low_side))
    def _():
        own_k_neg.start()
        own_edge.start()

    pl.semaphore_wait(barrier, COUNT - 1)

    near = place(jnp.bitwise_xor(me, 1))
    slip_out = pltpu.make_async_remote_copy(
        src_ref=slip.at[pl.ds((1 - rep) * LINES, LINES)],
        dst_ref=xin.at[rep],
        send_sem=sems.at[3],
        recv_sem=sems.at[4],
        device_id=near,
        device_id_type=MESH,
    )
    slip_out.start()

    mirror = place(COUNT - 1 - me)
    upper = spectrum.at[pl.ds(SLOTS, SLOTS)]
    k_to_pos = pltpu.make_async_remote_copy(
        src_ref=upper, dst_ref=pos, send_sem=sems.at[5], recv_sem=sems.at[6],
        device_id=mirror, device_id_type=MESH,
    )
    k_to_neg = pltpu.make_async_remote_copy(
        src_ref=upper, dst_ref=neg, send_sem=sems.at[5], recv_sem=sems.at[6],
        device_id=mirror, device_id_type=MESH,
    )
    edge_target = jnp.where(me == COUNT // 2, 0, COUNT - me)
    edge_out = pltpu.make_async_remote_copy(
        src_ref=spectrum.at[pl.ds(0, 1)], dst_ref=edge, send_sem=sems.at[7],
        recv_sem=sems.at[8], device_id=place(edge_target), device_id_type=MESH,
    )

    @pl.when(low_side)
    def _():
        k_to_pos.start()

    @pl.when(jnp.logical_not(low_side))
    def _():
        k_to_neg.start()
        edge_out.start()

    own_slip.wait()
    slip_out.wait_recv()

    def relay(col, carry):
        for side in range(2):
            lanes = pl.ds(pl.multiple_of(col * 128, 128), 128)
            xr[pl.ds(side * 32 + col, LINES, stride=64), :] = xin[side, :, lanes]
        return carry

    lax.fori_loop(0, 32, relay, 0, unroll=4)
    for name in NAMES:
        staged[name].wait()

    def strike(pair, carry):
        both = jnp.concatenate(
            [xr[pl.ds((2 * pair + i) * 64, 64), :] for i in range(2)], 1
        )
        out = table_dot(tab["t1"][...], both)
        cos, sin = tab["tw1c"][...], tab["tw1s"][...]
        for i in range(2):
            real = out[:64, i * 128 : (i + 1) * 128]
            imag = out[64:, i * 128 : (i + 1) * 128]
            yr[pl.ds(2 * pair + i, 64, stride=LINES), :] = real * cos + imag * sin
            yi[pl.ds(2 * pair + i, 64, stride=LINES), :] = imag * cos - real * sin
        return carry

    lax.fori_loop(0, LINES // 2, strike, 0, unroll=4)

    def exchange(src, dst, chunk, first_sem):
        mine = pl.ds(pl.multiple_of(me * ROWS, ROWS), ROWS)
        own_sem, send_sem, recv_sem = (chunk_sems.at[first_sem + i, chunk] for i in range(3))
        own = pltpu.make_async_copy(src.at[chunk, mine], dst.at[chunk, mine], own_sem)
        own.start()

        def send(step, carry):
            other = partner(step)
            pltpu.make_async_remote_copy(
                src_ref=src.at[chunk, pl.ds(pl.multiple_of(other * ROWS, ROWS), ROWS)],
                dst_ref=dst.at[chunk, mine],
                send_sem=send_sem,
                recv_sem=recv_sem,
                device_id=place(other),
                device_id_type=MESH,
            ).start()
            return carry

        lax.fori_loop(1, COUNT, send, 0)
        rest = pltpu.make_async_remote_copy(
            src_ref=src.at[chunk, pl.ds(0, (COUNT - 1) * ROWS)],
            dst_ref=dst.at[chunk, pl.ds(0, (COUNT - 1) * ROWS)],
            send_sem=send_sem,
            recv_sem=recv_sem,
            device_id=near,
            device_id_type=MESH,
        )
        return own, rest

    def second_stage(chunk, side, quad):
        first = (side * 32 + (chunk * QUADS + quad) * 4) * LINES
        rows = pl.ds(first, 256)
        out = table_dot_t(
            tab["t2b" if side else "t2a"][...], jnp.concatenate([yr[rows, :], yi[rows, :]], 1)
        )
        real, imag = out[:64], out[64:]
        if first == 0:
            high, low = split(yr[pl.ds(0, 128), :])
            alt = tab["alt"][...]
            extra = dot_t(alt, high) + dot_t(alt, low)
            lane = lax.broadcasted_iota(jnp.int32, (64, 128), 1)
            extra = jnp.where(lane < LINES, extra, 0.0)
            imag = jnp.concatenate([imag[:, :128] + extra, imag[:, 128:]], 1)
        for i in range(2):
            cols = slice(i * 128, (i + 1) * 128)
            start = side * 64 * ROWS + quad + i
            snd[chunk, pl.ds(start, 64, stride=ROWS), :] = real[:, cols]
            snd[chunk, pl.ds(start + QUADS, 64, stride=ROWS), :] = imag[:, cols]

    forward = []
    for chunk in range(CHUNKS):
        for side in range(2):
            for quad in range(0, QUADS, 2):
                second_stage(chunk, side, quad)
        forward.append(exchange(snd, rcv, chunk, 0))

    @pl.when(low_side)
    def _():
        own_k_pos.wait()
        k_to_neg.wait_recv()
        edge_out.wait_recv()

    @pl.when(jnp.logical_not(low_side))
    def _():
        own_k_neg.wait()
        own_edge.wait()
        k_to_pos.wait_recv()

    def fold(source, direct, back, rows, first):
        lane = lax.broadcasted_iota(jnp.int32, (rows, 128), 1)

        def load(tile):
            lanes = pl.ds(pl.multiple_of(tile * 128, 128), 128)
            return source[:, lanes] if rows < 8 else source[pl.ds(first, rows), lanes]

        base = first * 16 if rows >= 8 else SLOTS * 16

        def step(block, carry):
            for half in range(2):
                stride = dict(stride=16) if rows > 1 else {}
                direct[half, pl.ds(base + block, rows, **stride), :] = load(2 * block + half)
                value = load(32 + 2 * block + half)
                if half == 0:
                    after = load(jnp.minimum(32 + 2 * block + 2, 62))
                    after = jnp.where(block == 15, 0.0, after)
                    value = jnp.where(lane == 0, after, value)
                back[half, pl.ds(base + 15 - block, rows, **stride), :] = value
            return carry

        lax.fori_loop(0, 16, step, 0)

    fold(pos, pd, pr, SLOTS, 0)
    fold(neg, nd, nr, SLOTS, 0)
    fold(edge, nd, nr, 1, 0)

    def flip(back, rows):
        high, low = split(jnp.concatenate([back[0, rows, :], back[1, rows, :]], 1))
        return dot(high, tab["flip"][...]) + dot(low, tab["flip"][...])

    scale = 2.0 / (float(NS) * float(2 * ND))

    def combine(slot, carry):
        rows = pl.ds(pl.multiple_of(slot * 16, 16), 16)
        other = pl.ds(pl.multiple_of((SLOTS - slot) * 16, 16), 16)
        plus = jnp.concatenate([pd[0, rows, :], pd[1, rows, :]], 1)
        minus = jnp.concatenate([nd[0, other, :], nd[1, other, :]], 1)
        plus_back = flip(pr, rows)
        minus_back = flip(nr, other)
        packed = jnp.logical_and(me == 0, slot == 0)
        even_plus = (plus + plus_back) * scale
        even_minus = (minus + minus_back) * scale
        odd = ((plus - plus_back) - (minus - minus_back)) * scale
        both = even_plus + even_minus
        a_re[rows, :] = jnp.where(packed, even_plus, both)
        a_im[rows, :] = jnp.where(packed, even_minus, both)
        b_all[rows, :] = jnp.where(packed, 0.0, odd)
        return carry

    lax.fori_loop(0, SLOTS, combine, 0, unroll=4)

    def dip(chunk, quad, carry):
        got = jnp.concatenate(
            [rcv[chunk, pl.ds(comp * QUADS + quad, COUNT, stride=ROWS), :] for comp in range(2)], 1
        )
        first = table_dot(tab["t3"][...], got)
        cos, sin = tab["tw3c"][...], tab["tw3s"][...]
        spec = []
        for comp in range(2):
            real = first[:256, comp * 128 : (comp + 1) * 128]
            imag = first[256:, comp * 128 : (comp + 1) * 128]
            turned = jnp.concatenate([real * cos + imag * sin, imag * cos - real * sin], 1)
            spec.append(table_dot_t(tab["t4"][...], turned))
        rows = pl.ds(pl.multiple_of((chunk * QUADS + quad) * 64, 64), 64)
        b = b_all[rows, :]
        cos, sin = tab["tw5c"][...], tab["tw5s"][...]
        turned = []
        for even, odd in (
            (spec[0] * a_re[rows, :], spec[1] * b),
            (spec[1] * a_im[rows, :], -spec[0] * b),
        ):
            out = table_dot(tab["t5"][...], jnp.concatenate([even, odd], 0))
            real, imag = out[:128], out[128:]
            turned.append(
                jnp.concatenate([real * cos - imag * sin, real * sin + imag * cos], 1)
            )
        out = table_dot_t(tab["t6"][...], jnp.concatenate(turned, 0))
        for comp in range(2):
            snd2[chunk, pl.ds(comp * QUADS + quad, COUNT, stride=ROWS), :] = out[
                :, comp * 128 : (comp + 1) * 128
            ]
        return carry

    backward = []
    for chunk in range(CHUNKS):
        own, rest = forward[chunk]
        own.wait()
        rest.wait_recv()
        lax.fori_loop(0, QUADS, functools.partial(dip, chunk), 0, unroll=4)
        backward.append(exchange(snd2, rcv2, chunk, 3))

    def unstrike(chunk, side, quad, carry):
        start = side * 64 * ROWS + quad
        got = jnp.concatenate(
            [
                rcv2[chunk, pl.ds(start + comp * QUADS, 64, stride=ROWS), :]
                for comp in range(2)
            ],
            0,
        )
        high, low = split(got.T)
        out = dot(jnp.concatenate([high, low, high], 1), tab["t7b" if side else "t7a"][...])
        real, imag = out[:, :128], out[:, 128:]
        if side == 0 and chunk == 0:
            alt = tab["alt"][...]
            extra = dot(high[:, 64:], alt) + dot(low[:, 64:], alt)
            line = lax.broadcasted_iota(jnp.int32, (128, 128), 0)
            keep = jnp.logical_and(line < LINES, quad == 0)
            real = real + jnp.where(keep, extra, 0.0)
        for part in range(4):
            freq = side * 32 + (chunk * QUADS + quad) * 4 + part
            cos = tab["tw1c"][pl.ds(freq, 1), :]
            sin = tab["tw1s"][pl.ds(freq, 1), :]
            rows = pl.ds(pl.multiple_of(freq * LINES, LINES), LINES)
            r, i = real[part * 32 : part * 32 + 32], imag[part * 32 : part * 32 + 32]
            yr[rows, :] = r * cos - i * sin
            yi[rows, :] = r * sin + i * cos
        return carry

    for chunk in range(CHUNKS):
        own, rest = backward[chunk]
        own.wait()
        rest.wait_recv()
        for side in range(2):
            lax.fori_loop(
                0, QUADS, functools.partial(unstrike, chunk, side), 0, unroll=4
            )

    def last(pair, carry):
        both = jnp.concatenate(
            [
                jnp.concatenate(
                    [
                        yr[pl.ds(2 * pair + i, 64, stride=LINES), :],
                        yi[pl.ds(2 * pair + i, 64, stride=LINES), :],
                    ],
                    0,
                )
                for i in range(2)
            ],
            1,
        )
        out = table_dot(tab["t8"][...], both)
        for i in range(2):
            ebuf[pl.ds(2 * pair + i, 64, stride=LINES), :] = out[:, i * 128 : (i + 1) * 128]
        return carry

    def relay_back(first, side, dst, dst_first, col, carry):
        rows = pl.ds(pl.multiple_of((side * 32 + col) * LINES + first, 8), 8)
        lanes = pl.ds(pl.multiple_of(col * 128, 128), 128)
        dst[pl.ds(pl.multiple_of(dst_first, 8), 8), lanes] = ebuf[rows, :]
        return carry

    outgoing = []
    for part in range(LINES // 8):
        first = part * 8
        lax.fori_loop(part * 4, part * 4 + 4, last, 0, unroll=4)
        away = functools.partial(relay_back, first, 1 - rep, xout, first)
        lax.fori_loop(0, 32, away, 0, unroll=8)
        copy = pltpu.make_async_remote_copy(
            src_ref=xout.at[pl.ds(first, 8)],
            dst_ref=elastic.at[pl.ds(pl.multiple_of(rep * LINES + first, 8), 8)],
            send_sem=out_sems.at[0, part],
            recv_sem=out_sems.at[1, part],
            device_id=near,
            device_id_type=MESH,
        )
        copy.start()
        outgoing.append(copy)
    for part in range(LINES // 8):
        home = functools.partial(
            relay_back, part * 8, rep, elastic, rep * LINES + part * 8
        )
        lax.fori_loop(0, 32, home, 0, unroll=8)

    slip_out.wait_send()
    for own, rest in forward + backward:
        rest.wait_send()

    @pl.when(low_side)
    def _():
        k_to_pos.wait_send()

    @pl.when(jnp.logical_not(low_side))
    def _():
        k_to_neg.wait_send()
        edge_out.wait_send()

    for copy in outgoing:
        copy.wait()


def elastic_stress(slip_field, kernel_spectrum):
    made = tables()
    arrays = [jnp.asarray(made[name]) for name in NAMES]
    vmem = pl.BlockSpec(memory_space=pltpu.VMEM)
    flat = (64 * LINES, 128)
    packets = (CHUNKS, COUNT * ROWS, 128)
    return pl.pallas_call(
        body,
        out_shape=jax.ShapeDtypeStruct((64, 4096), F32),
        in_specs=[pl.BlockSpec(memory_space=pl.ANY)] * (2 + len(arrays)),
        out_specs=vmem,
        scratch_shapes=[pltpu.VMEM(a.shape, a.dtype) for a in arrays]
        + [pltpu.SemaphoreType.DMA((len(arrays),))]
        + [
            pltpu.VMEM((2, LINES, 4096), F32),
            pltpu.VMEM(flat, F32),
            pltpu.VMEM(flat, F32),
            pltpu.VMEM(flat, F32),
            pltpu.VMEM(packets, F32),
            pltpu.VMEM(packets, F32),
            pltpu.VMEM((SLOTS, 8192), F32),
            pltpu.VMEM((SLOTS, 8192), F32),
            pltpu.VMEM((1, 8192), F32),
            pltpu.VMEM((2, 512, 128), F32),
            pltpu.VMEM((2, 512, 128), F32),
            pltpu.VMEM((2, 528, 128), F32),
            pltpu.VMEM((2, 528, 128), F32),
            pltpu.VMEM((512, 256), F32),
            pltpu.VMEM((512, 256), F32),
            pltpu.VMEM((512, 256), F32),
            pltpu.VMEM(packets, F32),
            pltpu.VMEM(packets, F32),
            pltpu.VMEM(flat, F32),
            pltpu.VMEM((LINES, 4096), F32),
            pltpu.SemaphoreType.DMA((9,)),
            pltpu.SemaphoreType.DMA((6, CHUNKS)),
            pltpu.SemaphoreType.DMA((2, LINES // 8)),
        ],
        compiler_params=pltpu.CompilerParams(
            collective_id=1, has_side_effects=True, vmem_limit_bytes=60 * 2**20
        ),
        name="elastic_stress",
    )(slip_field, kernel_spectrum, *arrays)


def shards(slip_field, state_field, direct_effect, load_stress, kernel_spectrum):
    elastic = elastic_stress(slip_field, kernel_spectrum)
    stress = load_stress + elastic
    velocity = (
        2.0
        * jnp.sinh(stress / direct_effect)
        * jnp.exp(-state_exponent * jnp.log(state_field) / direct_effect)
    )
    state_next = (state_field + time_step) / (1.0 + time_step * jnp.abs(velocity))
    return (velocity, state_next)


def solution(mesh):
    placed = (
        P("dip", "rep"),
        P("dip", "rep"),
        P("dip", "rep"),
        P("dip", "rep"),
        P(("dip", "rep"), None),
    )
    return jax.shard_map(
        shards,
        mesh=mesh,
        in_specs=placed,
        out_specs=(P("dip", "rep"), P("dip", "rep")),
        check_vma=False,
    )
```

profile of v0, /device:TPU:1, one launch (start us, length us, event | category | flops | bytes accessed | tf_op | source)
XLA Modules:
  0.0 92.6 jit_solution(4899473209139675649)
XLA Ops:
  0.6 0.0 copy-start.2
  0.6 0.0 copy-start.1
  0.7 0.0 copy-start
  0.7 87.9 %elastic_stress.1 = f32[64,4096]{1,0:T(8,128)} custom-call(f32[64,4096]{1,0:T(8,128)} %slip.1, f32[64,8192]{1,0:T(8,128)} %spectrum.1, bf16[128,192]{1,0:T(8,128)(2,1)} %constant.46.clone.refs_0_, f32[64,128]{1,0:T(8,128)} %constant.47.clone.refs_1_, f32[64,128]{1,0:T(8,128)} %constant.48.clone.refs_2_, bf16[256,256]{1,0:T(8,128)(2,1)} %constant.49.clone.refs_3_, ...), custom_call_target="tpu_custom_call" | custom-call | tf_op jit(solution)/shard_map/elastic_stress/pallas_call | solution.py:509
  88.6 0.0 copy-done.2
  88.6 0.0 copy-done.1
  88.6 0.0 copy-done
  88.6 4.0 %add_divide_fusion = (f32[64,4096]{1,0:T(8,128)}, f32[64,4096]{1,0:T(8,128)}) fusion(f32[64,4096]{1,0:T(8,128)S(1)} %copy-done, f32[64,4096]{1,0:T(8,128)S(1)} %copy-done.1, f32[64,4096]{1,0:T(8,128)S(1)} %copy-done.2, f32[64,4096]{1,0:T(8,128)} %elastic_stress.1), kind=kLoop, calls=%fused_computation.5 | loop fusion | flops 5505024 | bytes 6291456 | tf_op jit(solution)/shard_map/div | solution.py:556
Async XLA Ops:
  0.6 88.0 %copy-start.2 = (f32[64,4096]{1,0:T(8,128)S(1)}, f32[64,4096]{1,0:T(8,128)}, u32[]{:S(2)}) copy-start(f32[64,4096]{1,0:T(8,128)} %param.26) | copy-start | bytes 3145732
  0.6 88.0 %copy-start.1 = (f32[64,4096]{1,0:T(8,128)S(1)}, f32[64,4096]{1,0:T(8,128)}, u32[]{:S(2)}) copy-start(f32[64,4096]{1,0:T(8,128)} %param.25) | copy-start | bytes 3145732
  0.7 88.0 %copy-start = (f32[64,4096]{1,0:T(8,128)S(1)}, f32[64,4096]{1,0:T(8,128)}, u32[]{:S(2)}) copy-start(f32[64,4096]{1,0:T(8,128)} %param.24) | copy-start | bytes 3145732
where the time goes:
time: 93.1 us; the launch traced here: 92.6 us
  Pallas kernels  87.9 us (94%)
  other arithmetic  3.97 us (4%)
    pallas_call x1, Pallas kernels, elastic_stress(): pl.pallas_call(body, out_shape=jax.ShapeDtypeStruct((64, 4096), F32), in_...  87.9 us
    div x1, other arithmetic, shards(): (state_field + time_step) / (1.0 + time_step * jnp.abs(velocity))  3.97 us

commit v1 on v0

--- a/solution.py
+++ b/solution.py
@@ -21,7 +21,8 @@
 COUNT = 128
 LINES = 32
 SLOTS = 32
-CHUNKS = 2
+CHUNKS = 4
+EARLY = 2
 QUADS = SLOTS // 4 // CHUNKS
 ROWS = 2 * QUADS
 
@@ -134,18 +135,17 @@
     }
     (
         xin, xr, yr, yi, snd, rcv, pos, neg, edge,
-        pd, pr, nd, nr, a_re, a_im, b_all, snd2, rcv2, ebuf, xout, sems, chunk_sems, out_sems,
+        pd, pr, nd, nr, a_re, a_im, b_all, snd2, rcv2, ebuf, xout, sems, k_sems, chunk_sems, out_sems,
     ) = refs[2 * count + 2 :]
     rep = lax.axis_index("rep")
     me = lax.axis_index("dip") * 2 + rep
     barrier = pltpu.get_barrier_semaphore()
 
     def place(other):
-        return (other // 2, other % 2)
+        return (lax.shift_right_logical(other, 1), jnp.bitwise_and(other, 1))
 
     def partner(step):
-        mixed = lax.rem(step * 37, COUNT - 1)
-        return jnp.bitwise_xor(me, jnp.where(mixed == 0, COUNT - 1, mixed))
+        return jnp.bitwise_xor(me, jnp.bitwise_and(step * 37, COUNT - 1))
 
     def greet(step, carry):
         pl.semaphore_signal(
@@ -187,29 +187,40 @@
     slip_out.start()
 
     mirror = place(COUNT - 1 - me)
-    upper = spectrum.at[pl.ds(SLOTS, SLOTS)]
-    k_to_pos = pltpu.make_async_remote_copy(
-        src_ref=upper, dst_ref=pos, send_sem=sems.at[5], recv_sem=sems.at[6],
-        device_id=mirror, device_id_type=MESH,
-    )
-    k_to_neg = pltpu.make_async_remote_copy(
-        src_ref=upper, dst_ref=neg, send_sem=sems.at[5], recv_sem=sems.at[6],
-        device_id=mirror, device_id_type=MESH,
-    )
+    part_rows = SLOTS // CHUNKS
+
+    def kernel_rows(chunk, dst, first):
+        return pltpu.make_async_remote_copy(
+            src_ref=spectrum.at[pl.ds(SLOTS + first, part_rows)],
+            dst_ref=dst.at[pl.ds(first, part_rows)],
+            send_sem=k_sems.at[0, chunk],
+            recv_sem=k_sems.at[1, chunk],
+            device_id=mirror,
+            device_id_type=MESH,
+        )
+
+    k_to_pos = [kernel_rows(c, pos, c * part_rows) for c in range(CHUNKS)]
+    k_to_neg = [kernel_rows(c, neg, SLOTS - (c + 1) * part_rows) for c in range(CHUNKS)]
     edge_target = jnp.where(me == COUNT // 2, 0, COUNT - me)
     edge_out = pltpu.make_async_remote_copy(
         src_ref=spectrum.at[pl.ds(0, 1)], dst_ref=edge, send_sem=sems.at[7],
         recv_sem=sems.at[8], device_id=place(edge_target), device_id_type=MESH,
     )
 
-    @pl.when(low_side)
-    def _():
-        k_to_pos.start()
-
-    @pl.when(jnp.logical_not(low_side))
-    def _():
-        k_to_neg.start()
-        edge_out.start()
+    def send_kernel_rows(first, stop):
+        @pl.when(low_side)
+        def _():
+            for copy in k_to_pos[first:stop]:
+                copy.start()
+
+        @pl.when(jnp.logical_not(low_side))
+        def _():
+            if first == 0:
+                edge_out.start()
+            for copy in k_to_neg[first:stop]:
+                copy.start()
+
+    send_kernel_rows(0, EARLY)
 
     own_slip.wait()
     slip_out.wait_recv()
@@ -294,18 +305,17 @@
             for quad in range(0, QUADS, 2):
                 second_stage(chunk, side, quad)
         forward.append(exchange(snd, rcv, chunk, 0))
+    send_kernel_rows(EARLY, CHUNKS)
 
     @pl.when(low_side)
     def _():
         own_k_pos.wait()
-        k_to_neg.wait_recv()
         edge_out.wait_recv()
 
     @pl.when(jnp.logical_not(low_side))
     def _():
         own_k_neg.wait()
         own_edge.wait()
-        k_to_pos.wait_recv()
 
     def fold(source, direct, back, rows, first):
         lane = lax.broadcasted_iota(jnp.int32, (rows, 128), 1)
@@ -328,10 +338,8 @@
                 back[half, pl.ds(base + 15 - block, rows, **stride), :] = value
             return carry
 
-        lax.fori_loop(0, 16, step, 0)
-
-    fold(pos, pd, pr, SLOTS, 0)
-    fold(neg, nd, nr, SLOTS, 0)
+        lax.fori_loop(0, 16, step, 0, unroll=4)
+
     fold(edge, nd, nr, 1, 0)
 
     def flip(back, rows):
@@ -357,7 +365,19 @@
         b_all[rows, :] = jnp.where(packed, 0.0, odd)
         return carry
 
-    lax.fori_loop(0, SLOTS, combine, 0, unroll=4)
+    def prepare(chunk):
+        @pl.when(low_side)
+        def _():
+            k_to_neg[chunk].wait_recv()
+
+        @pl.when(jnp.logical_not(low_side))
+        def _():
+            k_to_pos[chunk].wait_recv()
+
+        fold(pos, pd, pr, part_rows, chunk * part_rows)
+        fold(neg, nd, nr, part_rows, SLOTS - (chunk + 1) * part_rows)
+        first = chunk * part_rows
+        lax.fori_loop(first, first + part_rows, combine, 0, unroll=4)
 
     def dip(chunk, quad, carry):
         got = jnp.concatenate(
@@ -393,10 +413,11 @@
 
     backward = []
     for chunk in range(CHUNKS):
+        prepare(chunk)
         own, rest = forward[chunk]
         own.wait()
         rest.wait_recv()
-        lax.fori_loop(0, QUADS, functools.partial(dip, chunk), 0, unroll=4)
+        lax.fori_loop(0, QUADS, functools.partial(dip, chunk), 0, unroll=QUADS)
         backward.append(exchange(snd2, rcv2, chunk, 3))
 
     def unstrike(chunk, side, quad, carry):
@@ -433,7 +454,7 @@
         rest.wait_recv()
         for side in range(2):
             lax.fori_loop(
-                0, QUADS, functools.partial(unstrike, chunk, side), 0, unroll=4
+                0, QUADS, functools.partial(unstrike, chunk, side), 0, unroll=QUADS
             )
 
     def last(pair, carry):
@@ -489,11 +510,13 @@
 
     @pl.when(low_side)
     def _():
-        k_to_pos.wait_send()
+        for copy in k_to_pos:
+            copy.wait_send()
 
     @pl.when(jnp.logical_not(low_side))
     def _():
-        k_to_neg.wait_send()
+        for copy in k_to_neg:
+            copy.wait_send()
         edge_out.wait_send()
 
     for copy in outgoing:
@@ -535,6 +558,7 @@
             pltpu.VMEM(flat, F32),
             pltpu.VMEM((LINES, 4096), F32),
             pltpu.SemaphoreType.DMA((9,)),
+            pltpu.SemaphoreType.DMA((2, CHUNKS)),
             pltpu.SemaphoreType.DMA((6, CHUNKS)),
             pltpu.SemaphoreType.DMA((2, LINES // 8)),
         ],

time: 93.1 us -> 88.9 us (0.955)
  Pallas kernels: 87.9 us -> 84.1 us
    pallas_call x1, Pallas kernels: 87.9 us -> 84.1 us  [elastic_stress(): pl.pallas_call(body, out_shape=jax.ShapeDtypeStruct((64, 4096), F32), in_...]
where the time goes in v1:
time: 88.9 us; the launch traced here: 88.8 us
  Pallas kernels  84.1 us (95%)
  other arithmetic  3.97 us (4%)
    pallas_call x1, Pallas kernels, elastic_stress(): pl.pallas_call(body, out_shape=jax.ShapeDtypeStruct((64, 4096), F32), in_...  84.1 us
    div x1, other arithmetic, shards(): (state_field + time_step) / (1.0 + time_step * jnp.abs(velocity))  3.97 us

profile of v1, /device:TPU:1, one launch (start us, length us, event | category | flops | bytes accessed | tf_op | source)
XLA Modules:
  0.0 88.8 jit_solution(5642270590949701056)
XLA Ops:
  0.6 0.0 copy-start.2
  0.6 0.0 copy-start.1
  0.7 0.0 copy-start
  0.7 84.1 %elastic_stress.1 = f32[64,4096]{1,0:T(8,128)} custom-call(f32[64,4096]{1,0:T(8,128)} %slip.1, f32[64,8192]{1,0:T(8,128)} %spectrum.1, bf16[128,192]{1,0:T(8,128)(2,1)} %constant.46.clone.refs_0_, f32[64,128]{1,0:T(8,128)} %constant.47.clone.refs_1_, f32[64,128]{1,0:T(8,128)} %constant.48.clone.refs_2_, bf16[256,256]{1,0:T(8,128)(2,1)} %constant.49.clone.refs_3_, ...), custom_call_target="tpu_custom_call" | custom-call | tf_op jit(solution)/shard_map/elastic_stress/pallas_call | solution.py:532
  84.8 0.0 copy-done.2
  84.8 0.0 copy-done.1
  84.8 0.0 copy-done
  84.8 4.0 %add_divide_fusion = (f32[64,4096]{1,0:T(8,128)}, f32[64,4096]{1,0:T(8,128)}) fusion(f32[64,4096]{1,0:T(8,128)S(1)} %copy-done, f32[64,4096]{1,0:T(8,128)S(1)} %copy-done.1, f32[64,4096]{1,0:T(8,128)S(1)} %copy-done.2, f32[64,4096]{1,0:T(8,128)} %elastic_stress.1), kind=kLoop, calls=%fused_computation.5 | loop fusion | flops 5505024 | bytes 6291456 | tf_op jit(solution)/shard_map/div | solution.py:580
Async XLA Ops:
  0.6 84.1 %copy-start.2 = (f32[64,4096]{1,0:T(8,128)S(1)}, f32[64,4096]{1,0:T(8,128)}, u32[]{:S(2)}) copy-start(f32[64,4096]{1,0:T(8,128)} %param.26) | copy-start | bytes 3145732
  0.6 84.1 %copy-start.1 = (f32[64,4096]{1,0:T(8,128)S(1)}, f32[64,4096]{1,0:T(8,128)}, u32[]{:S(2)}) copy-start(f32[64,4096]{1,0:T(8,128)} %param.25) | copy-start | bytes 3145732
  0.7 84.1 %copy-start = (f32[64,4096]{1,0:T(8,128)S(1)}, f32[64,4096]{1,0:T(8,128)}, u32[]{:S(2)}) copy-start(f32[64,4096]{1,0:T(8,128)} %param.24) | copy-start | bytes 3145732

commit v2 on v1

--- a/solution.py
+++ b/solution.py
@@ -222,6 +222,40 @@
 
     send_kernel_rows(0, EARLY)
 
+    def fold(source, direct, back, rows, first):
+        lane = lax.broadcasted_iota(jnp.int32, (rows, 128), 1)
+
+        def load(tile):
+            lanes = pl.ds(pl.multiple_of(tile * 128, 128), 128)
+            return source[:, lanes] if rows < 8 else source[pl.ds(first, rows), lanes]
+
+        base = first * 16 if rows >= 8 else SLOTS * 16
+
+        def step(block, carry):
+            for half in range(2):
+                stride = dict(stride=16) if rows > 1 else {}
+                direct[half, pl.ds(base + block, rows, **stride), :] = load(2 * block + half)
+                value = load(32 + 2 * block + half)
+                if half == 0:
+                    after = load(jnp.minimum(32 + 2 * block + 2, 62))
+                    after = jnp.where(block == 15, 0.0, after)
+                    value = jnp.where(lane == 0, after, value)
+                back[half, pl.ds(base + 15 - block, rows, **stride), :] = value
+            return carry
+
+        lax.fori_loop(0, 16, step, 0, unroll=4)
+
+    @pl.when(low_side)
+    def _():
+        own_k_pos.wait()
+        fold(pos, pd, pr, SLOTS, 0)
+
+    @pl.when(jnp.logical_not(low_side))
+    def _():
+        own_k_neg.wait()
+        own_edge.wait()
+        fold(neg, nd, nr, SLOTS, 0)
+
     own_slip.wait()
     slip_out.wait_recv()
 
@@ -309,36 +343,7 @@
 
     @pl.when(low_side)
     def _():
-        own_k_pos.wait()
         edge_out.wait_recv()
-
-    @pl.when(jnp.logical_not(low_side))
-    def _():
-        own_k_neg.wait()
-        own_edge.wait()
-
-    def fold(source, direct, back, rows, first):
-        lane = lax.broadcasted_iota(jnp.int32, (rows, 128), 1)
-
-        def load(tile):
-            lanes = pl.ds(pl.multiple_of(tile * 128, 128), 128)
-            return source[:, lanes] if rows < 8 else source[pl.ds(first, rows), lanes]
-
-        base = first * 16 if rows >= 8 else SLOTS * 16
-
-        def step(block, carry):
-            for half in range(2):
-                stride = dict(stride=16) if rows > 1 else {}
-                direct[half, pl.ds(base + block, rows, **stride), :] = load(2 * block + half)
-                value = load(32 + 2 * block + half)
-                if half == 0:
-                    after = load(jnp.minimum(32 + 2 * block + 2, 62))
-                    after = jnp.where(block == 15, 0.0, after)
-                    value = jnp.where(lane == 0, after, value)
-                back[half, pl.ds(base + 15 - block, rows, **stride), :] = value
-            return carry
-
-        lax.fori_loop(0, 16, step, 0, unroll=4)
 
     fold(edge, nd, nr, 1, 0)
 
@@ -369,13 +374,13 @@
         @pl.when(low_side)
         def _():
             k_to_neg[chunk].wait_recv()
+            fold(neg, nd, nr, part_rows, SLOTS - (chunk + 1) * part_rows)
 
         @pl.when(jnp.logical_not(low_side))
         def _():
             k_to_pos[chunk].wait_recv()
-
-        fold(pos, pd, pr, part_rows, chunk * part_rows)
-        fold(neg, nd, nr, part_rows, SLOTS - (chunk + 1) * part_rows)
+            fold(pos, pd, pr, part_rows, chunk * part_rows)
+
         first = chunk * part_rows
         lax.fori_loop(first, first + part_rows, combine, 0, unroll=4)
 

time: 88.9 us -> 89 us (level)
  no operation moved by 1% of the time
where the time goes in v2:
time: 89 us; the launch traced here: 88.9 us
  Pallas kernels  84.2 us (95%)
  other arithmetic  3.97 us (4%)
    pallas_call x1, Pallas kernels, elastic_stress(): pl.pallas_call(body, out_shape=jax.ShapeDtypeStruct((64, 4096), F32), in_...  84.2 us
    div x1, other arithmetic, shards(): (state_field + time_step) / (1.0 + time_step * jnp.abs(velocity))  3.97 us

profile of v2, /device:TPU:1, one launch (start us, length us, event | category | flops | bytes accessed | tf_op | source)
XLA Modules:
  0.0 88.9 jit_solution(11469391505821737921)
XLA Ops:
  0.6 0.0 copy-start.2
  0.6 0.0 copy-start.1
  0.7 0.0 copy-start
  0.7 84.2 %elastic_stress.1 = f32[64,4096]{1,0:T(8,128)} custom-call(f32[64,4096]{1,0:T(8,128)} %slip.1, f32[64,8192]{1,0:T(8,128)} %spectrum.1, bf16[128,192]{1,0:T(8,128)(2,1)} %constant.46.clone.refs_0_, f32[64,128]{1,0:T(8,128)} %constant.47.clone.refs_1_, f32[64,128]{1,0:T(8,128)} %constant.48.clone.refs_2_, bf16[256,256]{1,0:T(8,128)(2,1)} %constant.49.clone.refs_3_, ...), custom_call_target="tpu_custom_call" | custom-call | tf_op jit(solution)/shard_map/elastic_stress/pallas_call | solution.py:537
  84.9 0.0 copy-done.2
  84.9 0.0 copy-done.1
  84.9 0.0 copy-done
  84.9 4.0 %add_divide_fusion = (f32[64,4096]{1,0:T(8,128)}, f32[64,4096]{1,0:T(8,128)}) fusion(f32[64,4096]{1,0:T(8,128)S(1)} %copy-done, f32[64,4096]{1,0:T(8,128)S(1)} %copy-done.1, f32[64,4096]{1,0:T(8,128)S(1)} %copy-done.2, f32[64,4096]{1,0:T(8,128)} %elastic_stress.1), kind=kLoop, calls=%fused_computation.5 | loop fusion | flops 5505024 | bytes 6291456 | tf_op jit(solution)/shard_map/div | solution.py:585
Async XLA Ops:
  0.6 84.2 %copy-start.2 = (f32[64,4096]{1,0:T(8,128)S(1)}, f32[64,4096]{1,0:T(8,128)}, u32[]{:S(2)}) copy-start(f32[64,4096]{1,0:T(8,128)} %param.26) | copy-start | bytes 3145732
  0.6 84.2 %copy-start.1 = (f32[64,4096]{1,0:T(8,128)S(1)}, f32[64,4096]{1,0:T(8,128)}, u32[]{:S(2)}) copy-start(f32[64,4096]{1,0:T(8,128)} %param.25) | copy-start | bytes 3145732
  0.7 84.2 %copy-start = (f32[64,4096]{1,0:T(8,128)S(1)}, f32[64,4096]{1,0:T(8,128)}, u32[]{:S(2)}) copy-start(f32[64,4096]{1,0:T(8,128)} %param.24) | copy-start | bytes 3145732
